TPU v7x, 256 devices: a whole 4x4x8 slice. The times are simulated.
256 devices in a mesh: dp: 8 (over x, y_lo), tm: 32 (over y_hi, z, core).
Axes of the slice: x: 4, y: 4 (y_hi: 2, y_lo: 2; y = y_hi * 2 + y_lo), z: 8, core: 2. Of those that a mesh axis runs over, the one named last changes fastest.
Arguments:
- frames: bfloat16 [8, 16384, 1536], P('dp', 'tm'), may hold values from -30 to 30
- lengths: int32 [8], P('dp'), may hold values from 8192 to 16384
- ln_gain: float32 [1536], replicated, may hold values from 0.1 to 1.9
- w_query: bfloat16 [1536, 1536], P(None, ('dp', 'tm')), may hold values from -1 to 1
- w_key: bfloat16 [1536, 1536], P(None, ('dp', 'tm')), may hold values from -1 to 1
- w_value: bfloat16 [1536, 1536], P(None, ('dp', 'tm')), may hold values from -0.15625 to 0.15625
- w_out: bfloat16 [1536, 1536], P(None, ('dp', 'tm')), may hold values from -0.15625 to 0.15625
Outputs:
- result: bfloat16 [8, 16384, 1536], P('dp', 'tm')
All inputs are finite; a program needn't handle non-finite values.
Results may differ from a plain program's by a relative error of at most 0.0033.
The roundings to bfloat16 on the way count: a program that leaves them out, or rounds other values in their place, can miss the bound.
Values may be sent and summed in bfloat16 or wider, within the bound.
A program may use at most 128 MiB of HBM per device.

v0:
```python
import math

import jax
import jax.numpy as jnp
from jax import lax
from jax.sharding import PartitionSpec as P

D = 1536
H = 16
HD = 96
W = 128


EPSILON = 1e-05


def with_halo(block, sides, width):
    for axis, dim in sides:
        count = lax.axis_size(axis)
        forward = [(i, i + 1) for i in range(count - 1)]
        backward = [(target, source) for source, target in forward]
        low = lax.ppermute(
            lax.slice_in_dim(block, block.shape[dim] - width, None, axis=dim), axis, forward
        )
        high = lax.ppermute(lax.slice_in_dim(block, 0, width, axis=dim), axis, backward)
        block = jnp.concatenate([low, block, high], axis=dim)
    return block


def norm_rows(values, ln_gain):
    as_float = values.astype(jnp.float32)
    row_mean = jnp.mean(as_float, axis=-1, keepdims=True)
    centered = as_float - row_mean
    row_var = jnp.mean(centered * centered, axis=-1, keepdims=True)
    return (centered * lax.rsqrt(row_var + EPSILON) * ln_gain).astype(jnp.bfloat16)


def apply_to(left_rows, pieces):
    return jnp.dot(left_rows, pieces, preferred_element_type=jnp.float32)


def attend(queries, key_ext, value_ext, first_pos, length):
    frame_count = queries.shape[0]
    tile_rows = math.gcd(frame_count, 512)
    num_tiles = frame_count // tile_rows
    scale = 1.0 / math.sqrt(HD)

    def attend_tile(tile_index):
        offset = tile_index * tile_rows
        query_tile = queries.reshape(tile_rows, H, HD)
        key_tile = key_ext.reshape(tile_rows + 2 * W, H, HD)
        value_tile = value_ext.reshape(tile_rows + 2 * W, H, HD)
        scores = (
            jnp.einsum("qhd,khd->hqk", query_tile, key_tile, preferred_element_type=jnp.float32)
            * scale
        )
        query_pos = first_pos + offset + jnp.arange(tile_rows, dtype=jnp.int32)
        key_pos = first_pos + offset - W + jnp.arange(tile_rows + 2 * W, dtype=jnp.int32)
        allowed = (
            (jnp.abs(query_pos[:, None] - key_pos[None, :]) <= W)
            & (key_pos >= 0)[None, :]
            & (key_pos < length)[None, :]
        )
        scores = scores + jnp.where(allowed, 0.0, -1000000000.0).astype(jnp.float32)[None]
        row_max = jnp.max(scores, axis=-1, keepdims=True)
        shifted = jnp.exp(scores - row_max)
        attn_probs = (shifted / jnp.sum(shifted, axis=-1, keepdims=True)).astype(jnp.bfloat16)
        attended = jnp.einsum(
            "hqk,khd->qhd", attn_probs, value_tile, preferred_element_type=jnp.float32
        )
        return attended.astype(jnp.bfloat16).reshape(tile_rows, D)

    tiles = lax.map(attend_tile, jnp.arange(num_tiles, dtype=jnp.int32))
    return tiles.reshape(frame_count, D)


def per_device(frames, lengths, ln_gain, w_query, w_key, w_value, w_out):
    own_frames = frames[0]
    frame_count = own_frames.shape[0]
    first_pos = lax.axis_index("tm") * frame_count
    normed = norm_rows(own_frames, ln_gain)
    queries = apply_to(normed, lax.all_gather(w_query, ("dp", "tm"), axis=1, tiled=True)).astype(
        jnp.bfloat16
    )
    key_rows = apply_to(normed, lax.all_gather(w_key, ("dp", "tm"), axis=1, tiled=True)).astype(
        jnp.bfloat16
    )
    value_rows = apply_to(normed, lax.all_gather(w_value, ("dp", "tm"), axis=1, tiled=True)).astype(
        jnp.bfloat16
    )
    stacked_kv = with_halo(jnp.stack([key_rows, value_rows]), (("tm", 1),), W)
    key_rows = stacked_kv[0]
    value_rows = stacked_kv[1]
    attended = attend(queries, key_rows, value_rows, first_pos, lengths[0])
    mixed_out = apply_to(attended, lax.all_gather(w_out, ("dp", "tm"), axis=1, tiled=True))
    summed = own_frames.astype(jnp.float32) + mixed_out
    is_valid = first_pos + jnp.arange(frame_count, dtype=jnp.int32) < lengths[0]
    result = jnp.where(is_valid[:, None], summed, 0.0).astype(jnp.bfloat16)
    return result[None]


def solution(mesh):
    in_specs = (
        P("dp", "tm", None),
        P("dp"),
        P(),
        P(None, ("dp", "tm")),
        P(None, ("dp", "tm")),
        P(None, ("dp", "tm")),
        P(None, ("dp", "tm")),
    )
    out_specs = P("dp", "tm", None)
    return jax.shard_map(
        per_device, mesh=mesh, in_specs=in_specs, out_specs=out_specs, check_vma=False
    )
```

profile of v0, /device:TPU:1, one launch (start us, length us, event | category | flops | bytes accessed | tf_op | source)
XLA Modules:
  0.0 1742.6 jit_solution(8797228680177882377)
XLA Ops:
  10.0 1.7 convert_reduce_fusion
  11.7 2.0 fusion.10
  13.7 1.8 fusion.20
  15.4 415.2 %all-gather.11.cloned.1.call-done = bf16[256,6,1536]{2,1,0:T(8,128)(2,1)} async-done(((bf16[1,6,1536]{2,1,0:T(8,128)(2,1)}), bf16[256,6,1536]{2,1,0:T(8,128)(2,1)}) %all-gather.11.cloned.1.call-update) | async-done | bytes 4718608 | tf_op jit(solution)/shard_map/all_gather | solution.py:88
  430.6 8.4 reshape.111
  439.0 409.4 %all-gather.9.cloned.1.call-done = bf16[256,6,1536]{2,1,0:T(8,128)(2,1)} async-done(((bf16[1,6,1536]{2,1,0:T(8,128)(2,1)}), bf16[256,6,1536]{2,1,0:T(8,128)(2,1)}) %all-gather.9.cloned.1.call-update) | async-done | bytes 4718608 | tf_op jit(solution)/shard_map/all_gather | solution.py:85
  848.4 8.4 reshape.109
  856.9 5.1 fusion.15
  862.0 2.7 fusion.14
  867.1 5.0 collective-permute-start.1
  872.1 2.3 collective-permute-start
  874.4 396.2 %all-gather.13.cloned.1.call-done = bf16[256,6,1536]{2,1,0:T(8,128)(2,1)} async-done(((bf16[1,6,1536]{2,1,0:T(8,128)(2,1)}), bf16[256,6,1536]{2,1,0:T(8,128)(2,1)}) %all-gather.13.cloned.1.call-update) | async-done | bytes 4718608 | tf_op jit(solution)/shard_map/all_gather | solution.py:82
  1270.6 8.4 reshape.113
  1279.0 6.2 convolution_convert_fusion
  1285.2 2.6 copy.15
  1287.8 399.3 %all-gather.15.cloned.1.call-done = bf16[256,6,1536]{2,1,0:T(8,128)(2,1)} async-done(((bf16[1,6,1536]{2,1,0:T(8,128)(2,1)}), bf16[256,6,1536]{2,1,0:T(8,128)(2,1)}) %all-gather.15.cloned.1.call-update) | async-done | bytes 4718608 | tf_op jit(solution)/shard_map/all_gather | solution.py:95
  1687.2 8.4 reshape.115
  1695.6 1.6 pad_maximum_fusion
  1697.2 1.7 fusion.29
  1698.9 4.3 copy.14
  1703.2 2.5 copy.16
  1705.7 15.3 fusion.30
  1721.0 11.2 fusion.17
  1732.2 3.9 fusion.16
  (34 shorter events, 5.2 us)
Async XLA Ops:
  6.5 424.1 %all-gather.11.cloned.1.call-start = ((), (), s32[]{:S(2)}) async-start(), calls=%async_computation.1 | async-start | bytes 6316032 | tf_op jit(solution)/shard_map/all_gather | solution.py:88
  7.3 841.1 %all-gather.9.cloned.1.call-start = ((), (), s32[]{:S(2)}) async-start(), calls=%async_computation | async-start | bytes 6316032 | tf_op jit(solution)/shard_map/all_gather | solution.py:85
  8.0 1262.6 %all-gather.13.cloned.1.call-start = ((), (), s32[]{:S(2)}) async-start(), calls=%async_computation.2 | async-start | bytes 6316032 | tf_op jit(solution)/shard_map/all_gather | solution.py:82
  8.7 1678.4 %all-gather.15.cloned.1.call-start = ((), (), s32[]{:S(2)}) async-start(), calls=%async_computation.3 | async-start | bytes 6316032 | tf_op jit(solution)/shard_map/all_gather | solution.py:95
  439.0 417.8 %copy-start = (bf16[1,512,1536]{2,1,0:T(8,128)(2,1)S(1)}, bf16[1,512,1536]{2,1,0:T(8,128)(2,1)}, u32[]{:S(2)}) copy-start(bf16[1,512,1536]{2,1,0:T(8,128)(2,1)} %param.7) | copy-start | bytes 4718596
  439.0 417.8 %copy-start.5 = (f32[1536]{0:T(1024)S(1)}, f32[1536]{0:T(1024)}, u32[]{:S(2)}) copy-start(f32[1536]{0:T(1024)} %param.9) | copy-start | bytes 18436
  856.8 5.2 copy-start.4
  864.7 1.1 copy-start.2
  867.1 828.5 %collective-permute-start.1 = (bf16[2,128,1536]{2,1,0:T(8,128)(2,1)}, bf16[2,128,1536]{2,1,0:T(8,128)(2,1)}, u32[]{:S(2)}, u32[]{:S(2)}) collective-permute-start(bf16[2,128,1536]{2,1,0:T(8,128)(2,1)} %get-tuple-element.20), channel_id=1, source_target_pairs={{1,0},{2,1},{3,2},{4,3},{5,4},{6,5},{7,6},{8,7},{9,8},{10,9},{11,1... | collective-permute-start | bytes 2359304 | tf_op jit(solution)/shard_map/ppermute | solution.py:25
  872.1 823.5 %collective-permute-start = (bf16[2,128,1536]{2,1,0:T(8,128)(2,1)}, bf16[2,128,1536]{2,1,0:T(8,128)(2,1)}, u32[]{:S(2)}, u32[]{:S(2)}) collective-permute-start(bf16[2,128,1536]{2,1,0:T(8,128)(2,1)} %get-tuple-element.19), channel_id=1, source_target_pairs={{0,1},{1,2},{2,3},{3,4},{4,5},{5,6},{6,7},{7,8},{8,9},{9,10},{10,1... | collective-permute-start | bytes 2359304 | tf_op jit(solution)/shard_map/ppermute | solution.py:22
  1287.8 407.7 %copy-start.3 = (bf16[1,512,1536]{2,1,0:T(8,128)(2,1)S(1)}, bf16[1,512,1536]{2,1,0:T(8,128)(2,1)}, u32[]{:S(2)}) copy-start(bf16[1,512,1536]{2,1,0:T(8,128)(2,1)} %copy-done.2) | copy-start | bytes 4718596
  1705.7 26.5 %slice-start = ((s8[4718592]{0:T(1024)(128)(4,1)}), s8[524288]{0:T(1024)(128)(4,1)S(1)}, s32[]{:S(2)}) async-start(s8[4718592]{0:T(1024)(128)(4,1)} %bitcast.62), calls=%async_computation.4 | async-start | bytes 1048576
  1721.0 11.2 copy-start.1
  1721.0 11.2 slice-start.1
Sparse Core Ops, SparseCore 0:
  9.2 421.3 all-gather.10
  432.5 415.8 all-gather.8
  850.3 420.2 all-gather.12
  1272.3 414.8 all-gather.14
where the time goes:
time: 1740 us
  waiting for transfers between devices  1620 us (93%)
  local copies, waits for them, and re-layouts  46 us (3%)
  matrix products  44.4 us (3%)
    all_gather x1, waiting for transfers between devices, per_device(): lax.all_gather(w_value, ('dp', 'tm'), axis=1, tiled=True)  415 us
    all_gather x1, waiting for transfers between devices, per_device(): lax.all_gather(w_key, ('dp', 'tm'), axis=1, tiled=True)  409 us
    all_gather x1, waiting for transfers between devices, per_device(): lax.all_gather(w_out, ('dp', 'tm'), axis=1, tiled=True)  399 us
    all_gather x1, waiting for transfers between devices, per_device(): lax.all_gather(w_query, ('dp', 'tm'), axis=1, tiled=True)  396 us
    unnamed x20, local copies, waits for them, and re-layouts  34.8 us
  transfers between devices with their start and end apart: 6, of which 4 were waited for; matrix products, arithmetic and copies ran while one was open for 3% of the time, Pallas kernels for 0%

commit v1 on v0

v1 whole, which is shorter than its diff:
```python
import math

import jax
import jax.numpy as jnp
from jax import lax
from jax.experimental import pallas as pl
from jax.experimental.pallas import tpu as pltpu
from jax.sharding import PartitionSpec as P

D = 1536
HALF = D // 2
H = 16
HD = 96
W = 128
ROWS = 512
EXT = ROWS + 2 * W
EPSILON = 1e-05
SCALE = 1.0 / math.sqrt(HD)
TQ = 256
TK = TQ + 2 * W
MESH = pl.DeviceIdType.MESH


def norm_rows(values, ln_gain):
    as_float = values.astype(jnp.float32)
    row_mean = jnp.mean(as_float, axis=-1, keepdims=True)
    centered = as_float - row_mean
    row_var = jnp.mean(centered * centered, axis=-1, keepdims=True)
    return (centered * lax.rsqrt(row_var + EPSILON) * ln_gain).astype(jnp.bfloat16)


def attend_head(q_t, k_t, v_t, bias_ref):
    pieces = []
    for t in range(ROWS // TQ):
        lo = t * TQ
        scores = lax.dot_general(
            k_t[:, lo : lo + TK],
            q_t[:, lo : lo + TQ],
            (((0,), (0,)), ((), ())),
            preferred_element_type=jnp.float32,
        )
        scores = scores * SCALE + bias_ref[t]
        shifted = jnp.exp(scores - jnp.max(scores, axis=0, keepdims=True))
        probs = (shifted * (1.0 / jnp.sum(shifted, axis=0, keepdims=True))).astype(jnp.bfloat16)
        pieces.append(
            jnp.dot(v_t[:, lo : lo + TK], probs, preferred_element_type=jnp.float32).astype(
                jnp.bfloat16
            )
        )
    return jnp.concatenate(pieces, axis=1)


def pick(index, options):
    value = options[0]
    for k, option in enumerate(options[1:], 1):
        value = jnp.where(index == k, option, value)
    return value


N_COPIES = 80


def body(len_ref, frames, gain_ref, pad_ref, out_ref, low, high, given, zbuf, w, obuf, wo, x_t, bias, att, send_sem, recv_sem):
    dp = lax.axis_index("dp")
    tm = lax.axis_index("tm")
    x, y = dp // 2, (tm // 16) * 2 + dp % 2
    z, core = (tm // 2) % 8, tm % 2

    def device(px, py, pz, pc):
        return (px * 2 + py % 2, (py // 2) * 16 + pz * 2 + pc)

    def moved(first, second):
        dx = jnp.where(core == 0, first, second)
        dy = jnp.where(core == 0, second, first)
        return (x + dx + 4) % 4, (y + dy + 4) % 4

    def plane_device(first, second):
        px, py = moved(first, second)
        return device(px, py, z, core)

    def plane_place(first, second):
        px, py = moved(first, second)
        return px * 4 + py

    partner = device(x, y, z, 1 - core)
    z_up, z_down = device(x, y, (z + 1) % 8, core), device(x, y, (z + 7) % 8, core)
    after, before = (dp, (tm + 1) % 32), (dp, (tm + 31) % 32)
    first_line = {k: plane_device(k, 0) for k in (-1, 1, 2)}
    second_line = {k: plane_device(0, k) for k in (-1, 1, 2)}
    peers = [*first_line.values(), *second_line.values(), z_up, z_down, partner, after, before]

    barrier = pltpu.get_barrier_semaphore()
    for peer in peers:
        pl.semaphore_signal(barrier, inc=1, device_id=peer, device_id_type=MESH)
    pl.semaphore_wait(barrier, len(peers))

    copies = {}

    def send(name, src, dst, peer):
        k = len(copies)
        copies[name] = pltpu.make_async_remote_copy(
            src_ref=src,
            dst_ref=dst,
            send_sem=send_sem.at[k],
            recv_sem=recv_sem.at[k],
            device_id=peer,
            device_id_type=MESH,
        )
        copies[name].start()

    def arrived(*names):
        for name in names:
            copies[name].wait_recv()

    send("swap", pad_ref.at[1 - core], given, partner)
    send("low", frames.at[pl.ds(ROWS - W, W)], low, after)
    send("high", frames.at[pl.ds(0, W)], high, before)

    first_pos = tm * ROWS
    length = len_ref[0]
    gain = gain_ref[...]

    def norm_block(ref, r, col):
        x_t[:, col : col + W] = norm_rows(ref[r : r + W], gain).T

    arrived("swap")
    mine, other = pad_ref[core], given[...]
    one = jnp.where(core == 0, mine, other)
    two = jnp.where(core == 0, other, mine)
    zbuf[z] = jnp.concatenate([one[:24], two[:24]], axis=0)
    own = plane_place(0, 0)
    obuf[core, z, own] = jnp.concatenate([one[24:], two[24:]], axis=0)

    send("zu1", zbuf.at[z], zbuf.at[z], z_up)
    send("zd1", zbuf.at[z], zbuf.at[z], z_down)
    for k in (-1, 1, 2):
        send(f"of{k}", obuf.at[core, z, own], obuf.at[core, z, own], first_line[k])

    norm_block(frames, 0, W)
    arrived("zu1", "zd1")
    for d in (2,):
        src = (z + 8 - (d - 1)) % 8
        send(f"zu{d}", zbuf.at[src], zbuf.at[src], z_up)
        src = (z + (d - 1)) % 8
        send(f"zd{d}", zbuf.at[src], zbuf.at[src], z_down)
    arrived("of-1", "of1", "of2")
    for i in (0, -1, 1, 2):
        place = plane_place(i, 0)
        for k in (-1, 1, 2):
            send(f"os{i},{k}", obuf.at[core, z, place], obuf.at[core, z, place], second_line[k])
    norm_block(frames, W, 2 * W)
    arrived("zu2", "zd2")
    src = (z + 6) % 8
    send("zu3", zbuf.at[src], zbuf.at[src], z_up)
    src = (z + 2) % 8
    send("zd3", zbuf.at[src], zbuf.at[src], z_down)
    norm_block(frames, 2 * W, 3 * W)
    arrived("zu3")
    src = (z + 5) % 8
    send("zu4", zbuf.at[src], zbuf.at[src], z_up)
    for i in (0, -1, 1, 2):
        arrived(*(f"os{i},{k}" for k in (-1, 1, 2)))
    send("ou1", obuf.at[core, z], obuf.at[core, z], z_up)
    send("od1", obuf.at[core, z], obuf.at[core, z], z_down)
    send("oc0", obuf.at[core, z], obuf.at[core, z], partner)
    norm_block(frames, 3 * W, 4 * W)
    arrived("zd3", "zu4")

    row = lax.broadcasted_iota(jnp.int32, (3 * HD, 8 * 48), 0)
    col = lax.broadcasted_iota(jnp.int32, (3 * HD, 8 * 48), 1)
    kind, unit, part = row // HD, (row % HD) // 6, row % 6
    source = (unit // 2) * 48 + (unit % 2) * 24 + kind * 8 + part
    order = jnp.where(col == source, 1.0, 0.0).astype(jnp.bfloat16)
    w[own, core] = jnp.dot(
        order, zbuf[...].reshape(8 * 48, HALF), preferred_element_type=jnp.float32
    ).astype(jnp.bfloat16)

    def slab(name, first, second, peer):
        ref = w.at[plane_place(first, second), core]
        send(name, ref, ref, peer)

    def lower(name, first, second, peer):
        ref = w.at[plane_place(first, second), core, pl.ds(0, 144)]
        send(name, ref, ref, peer)

    def upper(name, first, second, peer):
        ref = w.at[plane_place(first, second), core, pl.ds(144, 144)]
        send(name, ref, ref, peer)

    def share(first, second):
        slab(f"c{first},{second}", first, second, partner)

    share(0, 0)
    slab("f-", 0, 0, first_line[1])
    slab("f+", 0, 0, first_line[-1])
    slab("s0-", 0, 0, second_line[1])
    slab("s0+", 0, 0, second_line[-1])

    arrived("low", "high")
    norm_block(low, 0, 0)
    norm_block(high, 0, W + ROWS)
    for t in range(ROWS // TQ):
        key = lax.broadcasted_iota(jnp.int32, (TK, TQ), 0)
        query = lax.broadcasted_iota(jnp.int32, (TK, TQ), 1)
        key_pos = key + (first_pos + t * TQ - W)
        allowed = (
            (key - query >= 0) & (key - query <= 2 * W) & (key_pos >= 0) & (key_pos < length)
        )
        bias[t] = jnp.where(allowed, 0.0, -1e9).astype(jnp.float32)

    def heads(offsets):
        def one_head(k, carry):
            first = pick(k, [o[0] for o in offsets])
            second = pick(k, [o[1] for o in offsets])
            px, py = moved(first, second)
            place = px * 4 + py
            qkv = jnp.dot(w[place, 0], x_t[:HALF], preferred_element_type=jnp.float32)
            qkv += jnp.dot(w[place, 1], x_t[HALF:], preferred_element_type=jnp.float32)
            qkv = qkv.astype(jnp.bfloat16)
            att[px * 4 + (py % 2) * 2 + py // 2] = attend_head(
                qkv[:HD, W : W + ROWS], qkv[HD : 2 * HD], qkv[2 * HD :], bias
            )
            return carry

        lax.fori_loop(0, len(offsets), one_head, 0)

    def o_ring(d):
        arrived(f"ou{d}", f"od{d}")
        below, above = (z + 8 - d) % 8, (z + d) % 8
        if d < 3:
            send(f"ou{d + 1}", obuf.at[core, below], obuf.at[core, below], z_up)
            send(f"od{d + 1}", obuf.at[core, above], obuf.at[core, above], z_down)
        elif d == 3:
            ref = obuf.at[core, below, pl.ds(0, 8)]
            send("ou4", ref, ref, z_up)
            ref = obuf.at[core, above, pl.ds(8, 8)]
            send("od4", ref, ref, z_down)
        send(f"oc{d}", obuf.at[core, below], obuf.at[core, below], partner)
        if d < 4:
            send(f"oc-{d}", obuf.at[core, above], obuf.at[core, above], partner)

    arrived("c0,0")
    heads([(0, 0)])

    arrived("f-", "f+")
    lower("ff-", -1, 0, first_line[1])
    upper("ff+", 1, 0, first_line[-1])
    for i in (-1, 1):
        slab(f"s{i}-", i, 0, second_line[1])
        slab(f"s{i}+", i, 0, second_line[-1])
        share(i, 0)

    def second_step(i):
        arrived(f"s{i}-", f"s{i}+")
        lower(f"ss{i}-", i, -1, second_line[1])
        upper(f"ss{i}+", i, 1, second_line[-1])
        share(i, -1)
        share(i, 1)

    def second_end(i):
        arrived(f"ss{i}-", f"ss{i}+")
        share(i, 2)

    second_step(0)
    o_ring(1)
    arrived("c-1,0", "c1,0", "c0,-1", "c0,1")
    heads([(-1, 0), (1, 0)])
    arrived("ff-", "ff+")
    slab("s2-", 2, 0, second_line[1])
    slab("s2+", 2, 0, second_line[-1])
    share(2, 0)
    second_end(0)
    heads([(0, -1), (0, 1)])
    o_ring(2)
    arrived("c2,0", "c0,2")
    heads([(2, 0), (0, 2)])
    second_step(-1)
    second_step(1)
    o_ring(3)
    arrived("c-1,-1", "c-1,1", "c1,-1", "c1,1")
    heads([(-1, -1), (1, 1), (-1, 1), (1, -1)])
    second_step(2)
    second_end(-1)
    second_end(1)
    o_ring(4)
    arrived("c2,-1", "c2,1", "c-1,2", "c1,2")
    heads([(2, -1), (2, 1), (-1, 2), (1, 2)])
    second_end(2)

    arrived("oc0", "oc1", "oc2", "oc3", "oc4", "oc-1", "oc-2", "oc-3")
    row = lax.broadcasted_iota(jnp.int32, (HD, 8 * 16), 0)
    col = lax.broadcasted_iota(jnp.int32, (HD, 8 * 16), 1)
    unit, part = row // 6, row % 6
    order = jnp.where(col == unit * 8 + part, 1.0, 0.0).astype(jnp.bfloat16)
    for h in range(H):
        place = (h // 4) * 4 + (h % 2) * 2 + (h // 2) % 2
        for half in range(2):
            wo[h, :, half * HALF : (half + 1) * HALF] = jnp.dot(
                order,
                obuf[half, :, place].reshape(8 * 16, HALF),
                preferred_element_type=jnp.float32,
            ).astype(jnp.bfloat16)
    arrived("c2,2")
    heads([(2, 2)])

    att_rows = att[...].reshape(D, ROWS).T
    pos = first_pos + lax.broadcasted_iota(jnp.int32, (ROWS, 1), 0)
    for c in range(0, H, 4):
        mixed = lax.dot_general(
            att_rows,
            wo[c : c + 4].reshape(4 * HD, D),
            (((1,), (1,)), ((), ())),
            preferred_element_type=jnp.float32,
        )
        cols = slice(c * HD, (c + 4) * HD)
        summed = frames[:, cols].astype(jnp.float32) + mixed
        out_ref[:, cols] = jnp.where(pos < length, summed, 0.0).astype(jnp.bfloat16)

    for copy in copies.values():
        copy.wait_send()
    assert len(copies) <= N_COPIES


def per_device(frames, lengths, ln_gain, w_query, w_key, w_value, w_out):
    stack = jnp.stack([w.T for w in (w_query, w_key, w_value, w_out)])
    padded = jnp.pad(stack, ((0, 0), (0, 2), (0, 0))).reshape(32, 2, HALF).transpose(1, 0, 2)
    vmem = pl.BlockSpec(memory_space=pltpu.VMEM)
    bf16 = jnp.bfloat16
    result = pl.pallas_call(
        body,
        out_shape=jax.ShapeDtypeStruct((ROWS, D), bf16),
        in_specs=[pl.BlockSpec(memory_space=pltpu.SMEM), vmem, vmem, vmem],
        out_specs=vmem,
        scratch_shapes=[
            pltpu.VMEM((W, D), bf16),
            pltpu.VMEM((W, D), bf16),
            pltpu.VMEM((32, HALF), bf16),
            pltpu.VMEM((8, 48, HALF), bf16),
            pltpu.VMEM((H, 2, 3 * HD, HALF), bf16),
            pltpu.VMEM((2, 8, H, 16, HALF), bf16),
            pltpu.VMEM((H, HD, D), bf16),
            pltpu.VMEM((D, EXT), bf16),
            pltpu.VMEM((ROWS // TQ, TK, TQ), jnp.float32),
            pltpu.VMEM((H, HD, ROWS), bf16),
            pltpu.SemaphoreType.DMA((N_COPIES,)),
            pltpu.SemaphoreType.DMA((N_COPIES,)),
        ],
        compiler_params=pltpu.CompilerParams(
            collective_id=0, has_side_effects=True, vmem_limit_bytes=60 * 2**20
        ),
    )(lengths, frames[0], ln_gain[None], padded)
    return result[None]


def solution(mesh):
    in_specs = (
        P("dp", "tm", None),
        P("dp"),
        P(),
        P(None, ("dp", "tm")),
        P(None, ("dp", "tm")),
        P(None, ("dp", "tm")),
        P(None, ("dp", "tm")),
    )
    return jax.shard_map(
        per_device,
        mesh=mesh,
        in_specs=in_specs,
        out_specs=P("dp", "tm", None),
        check_vma=False,
    )
```

time: 1740 us -> 105 us (0.06)
  waiting for transfers between devices: 1620 us -> 0 us
  Pallas kernels: 0 us -> 98.5 us
  matrix products: 44.4 us -> 0 us
  local copies, waits for them, and re-layouts: 46 us -> 4.63 us
    all_gather x4 -> x0, waiting for transfers between devices: 1620 us -> none  [the longest x1 415 us: per_device(): lax.all_gather(w_value, ('dp', 'tm'), axis=1, tiled=True)]
    pallas_call x0 -> x1, Pallas kernels: none -> 98.5 us  [per_device(): pl.pallas_call(body, out_shape=jax.ShapeDtypeStruct((ROWS, D), bf16), in_...]
    unnamed x20 -> x1, local copies, waits for them, and re-layouts: 34.8 us -> 2.65 us
    dot_general x5 -> x0, matrix products: 29.1 us -> none  [the longest x4 17.9 us: apply_to(): return jnp.dot(left_rows, pieces, preferred_element_type=jnp.float32)]
  transfers between devices with their start and end apart: 6 -> 0, of which waited for: 4 -> 0; matrix products, arithmetic and copies ran while one was open for 3% -> 0% of each run, Pallas kernels for 0% -> 0%
where the time goes in v1:
time: 105 us
  Pallas kernels  98.5 us (94%)
  local copies, waits for them, and re-layouts  4.63 us (4%)
    pallas_call x1, Pallas kernels, per_device(): pl.pallas_call(body, out_shape=jax.ShapeDtypeStruct((ROWS, D), bf16), in_...  98.5 us
    unnamed x1, local copies, waits for them, and re-layouts  2.65 us

profile of v1, /device:TPU:1, one launch (start us, length us, event | category | flops | bytes accessed | tf_op | source)
XLA Modules:
  0.0 104.7 jit_solution(1776854038650955613)
XLA Ops:
  0.7 1.3 %broadcast_in_dim.6.gain_ref = f32[1,1536]{1,0:T(1,128)} reshape(f32[1536]{0:T(1024)} %param.9) | data formatting | bytes 12288 | tf_op jit(solution)/shard_map/broadcast_in_dim | solution.py:351
  1.9 0.8 fusion.6
  2.8 0.7 copy.10
  3.5 98.5 %shard_map.73 = bf16[512,1536]{1,0:T(8,128)(2,1)} custom-call(s32[1]{0:T(128)S(6)} %copy.12.len_ref, bf16[512,1536]{1,0:T(8,128)(2,1)} %bitcast.18, f32[1,1536]{1,0:T(1,128)} %broadcast_in_dim.6.gain_ref, bf16[2,32,768]{2,1,0:T(8,128)(2,1)} %bitcast.19), custom_call_target="tpu_custom_call" | custom-call | tf_op jit(solution)/shard_map/pallas_call | solution.py:329
  102.0 2.7 %copy.13 = bf16[1,512,1536]{2,1,0:T(8,128)(2,1)} copy(bf16[1,512,1536]{2,1,0:T(8,128)(2,1)} %bitcast.17) | data formatting | bytes 3145728
  (1 shorter events, 0.0 us)

commit v2 on v1

v2 whole, which is shorter than its diff:
```python
import math

import jax
import jax.numpy as jnp
from jax import lax
from jax.experimental import pallas as pl
from jax.experimental.pallas import tpu as pltpu
from jax.sharding import PartitionSpec as P

D = 1536
HALF = D // 2
H = 16
HD = 96
W = 128
ROWS = 512
EXT = ROWS + 2 * W
EPSILON = 1e-05
SCALE = 1.0 / math.sqrt(HD)
TQ = 256
TK = TQ + 2 * W
MESH = pl.DeviceIdType.MESH


def norm_rows(values, ln_gain):
    as_float = values.astype(jnp.float32)
    row_mean = jnp.mean(as_float, axis=-1, keepdims=True)
    centered = as_float - row_mean
    row_var = jnp.mean(centered * centered, axis=-1, keepdims=True)
    return (centered * lax.rsqrt(row_var + EPSILON) * ln_gain).astype(jnp.bfloat16)


def attend_head(q_t, k_t, v_t, bias_ref):
    pieces = []
    blank = jnp.zeros((W, W), jnp.bfloat16)
    for t in range(ROWS // TQ):
        lo = t * TQ
        scores = lax.dot_general(
            k_t[:, lo : lo + TK],
            q_t[:, lo : lo + TQ],
            (((0,), (0,)), ((), ())),
            preferred_element_type=jnp.float32,
        )
        sides = []
        for n in range(2):
            part = scores[n * W : n * W + 3 * W, n * W : n * W + W]
            part = part * (SCALE * math.log2(math.e)) + bias_ref[2 * t + n]
            shifted = jnp.exp2(part - jnp.max(part, axis=0, keepdims=True))
            probs = shifted * (1.0 / jnp.sum(shifted, axis=0, keepdims=True))
            probs = probs.astype(jnp.bfloat16)
            sides.append(jnp.concatenate([blank, probs] if n else [probs, blank], axis=0))
        probs = jnp.concatenate(sides, axis=1)
        pieces.append(
            jnp.dot(v_t[:, lo : lo + TK], probs, preferred_element_type=jnp.float32).astype(
                jnp.bfloat16
            )
        )
    return jnp.concatenate(pieces, axis=1)


def pick(index, options):
    value = options[0]
    for k, option in enumerate(options[1:], 1):
        value = jnp.where(index == k, option, value)
    return value


N_COPIES = 128
LINE = (-1, 1, 2)
KEYS, REST = 0, 1
PART_ROWS = (HD, 2 * HD)


def body(len_ref, frames_hbm, gain_ref, wk_ref, wv_ref, wq_ref, wo_ref, out_hbm, frames, out, raw, pad, low, high, given, zk, zr, wk, wr, oline, obuf, wo, x_t, kbuf, bias, att, in_sem, out_sem, send_sem, recv_sem):
    dp = lax.axis_index("dp")
    tm = lax.axis_index("tm")
    x, y = dp // 2, (tm // 16) * 2 + dp % 2
    z, core = (tm // 2) % 8, tm % 2

    def device(px, py, pz, pc):
        return (px * 2 + py % 2, (py // 2) * 16 + pz * 2 + pc)

    def moved(first, second):
        dx = jnp.where(core == 0, first, second)
        dy = jnp.where(core == 0, second, first)
        return (x + dx + 4) % 4, (y + dy + 4) % 4

    def plane_device(first, second):
        px, py = moved(first, second)
        return device(px, py, z, core)

    def plane_place(first, second):
        px, py = moved(first, second)
        return px * 4 + py

    partner = device(x, y, 1 * z, 1 - core)
    z_line = {k: device(x, y, (z + k + 8) % 8, core) for k in (4, 3, -3, 2, -2, 1, -1)}
    after, before = (dp, (tm + 1) % 32), (dp, (tm + 31) % 32)
    first_line = {k: plane_device(k, 0) for k in LINE}
    second_line = {k: plane_device(0, k) for k in LINE}
    peers = [*first_line.values(), *second_line.values(), *z_line.values(), partner, after, before]

    fetch = pltpu.make_async_copy(frames_hbm, frames, in_sem)
    fetch.start()
    barrier = pltpu.get_barrier_semaphore()
    for peer in peers:
        pl.semaphore_signal(barrier, inc=1, device_id=peer, device_id_type=MESH)

    raw[...] = jnp.zeros_like(raw)
    for n, ref in enumerate((wk_ref, wv_ref, wq_ref, wo_ref)):
        raw[8 * n : 8 * n + 6] = ref[...].astype(jnp.float32)
    pad[0] = raw[:, :HALF].astype(jnp.bfloat16)
    pad[1] = raw[:, HALF:].astype(jnp.bfloat16)
    pl.semaphore_wait(barrier, len(peers))

    copies = {}

    def send(name, src, dst, peer):
        k = len(copies)
        copies[name] = pltpu.make_async_remote_copy(
            src_ref=src,
            dst_ref=dst,
            send_sem=send_sem.at[k],
            recv_sem=recv_sem.at[k],
            device_id=peer,
            device_id_type=MESH,
        )
        copies[name].start()

    def arrived(*names):
        for name in names:
            copies[name].wait_recv()

    send("swap", pad.at[1 - core], given, partner)

    first_pos = tm * ROWS
    length = len_ref[0]
    gain = gain_ref[...].reshape(1, D)

    def norm_block(ref, r, col):
        x_t[:, col : col + W] = norm_rows(ref[r : r + W], gain).T

    arrived("swap")
    mine, other = pad[core], given[...]
    one = jnp.where(core == 0, mine, other)
    two = jnp.where(core == 0, other, mine)
    own = plane_place(0, 0)
    zk[z] = jnp.concatenate([one[:8], two[:8]], axis=0)
    for k, peer in z_line.items():
        send(f"zk{k}", zk.at[z], zk.at[z], peer)
    along = jnp.where(core == 0, x, y)
    across = jnp.where(core == 0, y, x)
    oline[along] = jnp.concatenate([one[24:], two[24:]], axis=0)
    for k in LINE:
        send(f"of{k}", oline.at[along], oline.at[along], first_line[k])
    zr[z] = jnp.concatenate([one[8:24], two[8:24]], axis=0)
    fetch.wait()

    norm_block(frames, 0, W)
    norm_block(frames, W, 2 * W)

    def ordered(buf, kinds):
        rows, cols = kinds * HD, 8 * kinds * 16
        row = lax.broadcasted_iota(jnp.int32, (rows, cols), 0)
        col = lax.broadcasted_iota(jnp.int32, (rows, cols), 1)
        kind, unit, part = row // HD, (row % HD) // 6, row % 6
        source = (unit // 2) * (kinds * 16) + (unit % 2) * (kinds * 8) + kind * 8 + part
        order = jnp.where(col == source, 1.0, 0.0).astype(jnp.bfloat16)
        return jnp.dot(order, buf.reshape(cols, HALF), preferred_element_type=jnp.float32).astype(
            jnp.bfloat16
        )

    parts = (wk, wr)

    def slab(name, part, first, second, peer, lo=0, size=None):
        ref = parts[part].at[plane_place(first, second), core]
        if size is not None:
            ref = parts[part].at[plane_place(first, second), core, pl.ds(lo, size)]
        send(f"{name},{part}", ref, ref, peer)

    def share(part, first, second):
        slab(f"c{first},{second}", part, first, second, partner)

    def begin(part):
        slab("f-", part, 0, 0, first_line[1])
        slab("f+", part, 0, 0, first_line[-1])
        slab("s0-", part, 0, 0, second_line[1])
        slab("s0+", part, 0, 0, second_line[-1])
        share(part, 0, 0)

    def first_step(part):
        half = PART_ROWS[part] // 2
        arrived(f"f-,{part}", f"f+,{part}")
        slab("ff-", part, -1, 0, first_line[1], 0, half)
        slab("ff+", part, 1, 0, first_line[-1], half, half)
        share(part, -1, 0)
        share(part, 1, 0)

    def second_begin(part, i):
        slab(f"s{i}-", part, i, 0, second_line[1])
        slab(f"s{i}+", part, i, 0, second_line[-1])

    def first_end(part):
        arrived(f"ff-,{part}", f"ff+,{part}")
        share(part, 2, 0)

    def second_step(part, i):
        half = PART_ROWS[part] // 2
        arrived(f"s{i}-,{part}", f"s{i}+,{part}")
        slab(f"ss{i}-", part, i, -1, second_line[1], 0, half)
        slab(f"ss{i}+", part, i, 1, second_line[-1], half, half)
        share(part, i, -1)
        share(part, i, 1)

    def second_end(part, i):
        arrived(f"ss{i}-,{part}", f"ss{i}+,{part}")
        share(part, i, 2)

    def locate(k, offsets, n, together):
        first = pick(k, [o[0] for o in offsets[n::together]])
        second = pick(k, [o[1] for o in offsets[n::together]])
        px, py = moved(first, second)
        return px * 4 + py, px * 4 + (py % 2) * 2 + py // 2

    def project(ref, places):
        rows = jnp.concatenate(
            [jnp.concatenate([ref[place, 0], ref[place, 1]], axis=1) for place in places], axis=0
        )
        return jnp.dot(rows, x_t[...], preferred_element_type=jnp.float32).astype(jnp.bfloat16)

    def keys(*offsets):
        arrived(*(f"c{second},{first},{KEYS}" for first, second in offsets))

        def some_keys(k, carry):
            places, names = zip(*(locate(k, offsets, n, 2) for n in range(2)))
            k_t = project(wk, places)
            for n in range(2):
                kbuf[names[n]] = k_t[n * HD : (n + 1) * HD]
            return carry

        lax.fori_loop(0, len(offsets) // 2, some_keys, 0)

    def heads(*offsets):
        arrived(*(f"c{second},{first},{REST}" for first, second in offsets))
        together = 2 - len(offsets) % 2

        def some_heads(k, carry):
            places, names = zip(*(locate(k, offsets, n, together) for n in range(together)))
            vq = project(wr, places)
            for n in range(together):
                v_t, q_t = (vq[(2 * n + m) * HD : (2 * n + m + 1) * HD] for m in range(2))
                att[names[n]] = attend_head(q_t[:, W : W + ROWS], kbuf[names[n]], v_t, bias)
            return carry

        lax.fori_loop(0, len(offsets) // together, some_heads, 0)

    def o_send(name, place, half, peer):
        ref = obuf.at[core, place, pl.ds(2 * half, 2)]
        send(f"{name}{half}", ref, ref, peer)

    def o_share(k):
        ref = obuf.at[core, (z + k + 8) % 8]
        send(f"oc{k}", ref, ref, partner)

    def o_begin():
        arrived(*(f"os{k}" for k in LINE))
        for half in range(2):
            o_send("ou1.", z, half, z_line[1])
            o_send("od1.", z, half, z_line[-1])
        o_share(0)

    def o_ring(d, half):
        arrived(f"ou{d}.{half}", f"od{d}.{half}")
        below, above = (z + 8 - d) % 8, (z + d) % 8
        if d < 3 or half == 0:
            o_send(f"ou{d + 1}.", below, half, z_line[1])
        if d < 3 or half == 1:
            o_send(f"od{d + 1}.", above, half, z_line[-1])
        if half == 1:
            o_share(-d)
            o_share(d)

    def o_end():
        arrived("ou4.0", "od4.1")
        o_share(4)

    arrived(*(f"zk{k}" for k in z_line))
    for k, peer in z_line.items():
        send(f"zr{k}", zr.at[z], zr.at[z], peer)
    wk[own, core] = ordered(zk[...], 1)
    begin(KEYS)
    arrived(*(f"of{k}" for k in LINE))
    row = lax.broadcasted_iota(jnp.int32, (48, 64), 0)
    col = lax.broadcasted_iota(jnp.int32, (48, 64), 1)
    order = jnp.where(col == (row // 6) * 8 + row % 6, 1.0, 0.0).astype(jnp.bfloat16)
    obuf[core, z, across] = jnp.dot(
        order, oline[...].reshape(64, HALF), preferred_element_type=jnp.float32
    ).astype(jnp.bfloat16)
    for k in LINE:
        send(f"os{k}", obuf.at[core, z, across], obuf.at[core, z, across], second_line[k])
    norm_block(frames, 2 * W, 3 * W)
    first_step(KEYS)
    second_step(KEYS, 0)
    second_begin(KEYS, -1)
    second_begin(KEYS, 1)
    norm_block(frames, 3 * W, 4 * W)
    arrived(*(f"zr{k}" for k in z_line))
    wr[own, core] = ordered(zr[...], 2)
    begin(REST)
    send("low", frames_hbm.at[pl.ds(ROWS - W, W)], low, after)
    send("high", frames_hbm.at[pl.ds(0, W)], high, before)
    o_begin()
    first_end(KEYS)
    second_begin(KEYS, 2)
    second_end(KEYS, 0)
    for t in range(ROWS // W):
        key = lax.broadcasted_iota(jnp.int32, (3 * W, W), 0)
        query = lax.broadcasted_iota(jnp.int32, (3 * W, W), 1)
        key_pos = key + (first_pos + (t - 1) * W)
        allowed = (
            (key - query >= 0) & (key - query <= 2 * W) & (key_pos >= 0) & (key_pos < length)
        )
        bias[t] = jnp.where(allowed, 0.0, -1e9).astype(jnp.float32)
    arrived("low", "high")
    norm_block(low, 0, 0)
    norm_block(high, 0, W + ROWS)
    second_step(KEYS, -1)
    second_step(KEYS, 1)
    o_ring(1, 0)
    keys((0, 0), (-1, 0), (1, 0), (0, -1), (0, 1), (2, 0))
    o_ring(1, 1)
    first_step(REST)
    second_step(REST, 0)
    second_begin(REST, -1)
    second_begin(REST, 1)
    second_step(KEYS, 2)
    second_end(KEYS, -1)
    second_end(KEYS, 1)
    heads((0, 0))
    o_ring(2, 0)
    keys((0, 2), (-1, -1), (1, 1), (-1, 1))
    second_end(KEYS, 2)
    o_ring(2, 1)
    first_end(REST)
    second_begin(REST, 2)
    second_end(REST, 0)
    heads((-1, 0), (1, 0))
    o_ring(3, 0)
    heads((0, -1), (0, 1))
    second_step(REST, -1)
    o_ring(3, 1)
    keys((1, -1), (2, -1), (2, 1), (-1, 2), (1, 2), (2, 2))
    second_step(REST, 1)
    heads((2, 0), (0, 2))
    o_end()
    second_end(REST, -1)
    heads((-1, -1), (1, 1))
    second_step(REST, 2)
    second_end(REST, 1)
    heads((-1, 1), (1, -1))
    arrived(*(f"oc{k}" for k in range(-3, 5)))
    row = lax.broadcasted_iota(jnp.int32, (4 * HD, 8 * 48), 0)
    col = lax.broadcasted_iota(jnp.int32, (4 * HD, 8 * 48), 1)
    unit, part = (row % HD) // 12, row % 12
    order = jnp.where(col == unit * 48 + (row // HD) * 12 + part, 1.0, 0.0).astype(jnp.bfloat16)
    for half in range(2):
        for fixed in range(4):
            four = jnp.dot(
                order,
                obuf[half, :, fixed].reshape(8 * 48, HALF),
                preferred_element_type=jnp.float32,
            ).astype(jnp.bfloat16)
            for k in range(4):
                px, py = (fixed, k) if half else (k, fixed)
                head = px * 4 + (py % 2) * 2 + py // 2
                wo[head, :, half * HALF : (half + 1) * HALF] = four[k * HD : (k + 1) * HD]
    heads((2, -1), (-1, 2))
    second_end(REST, 2)
    heads((2, 1), (1, 2))
    heads((2, 2))

    att_rows = att[...].reshape(D, ROWS).T
    pos = first_pos + lax.broadcasted_iota(jnp.int32, (ROWS, 1), 0)
    stores = []
    for n, c in enumerate(range(0, H, 4)):
        mixed = lax.dot_general(
            att_rows,
            wo[c : c + 4].reshape(4 * HD, D),
            (((1,), (1,)), ((), ())),
            preferred_element_type=jnp.float32,
        )
        cols = pl.ds(c * HD, 4 * HD)
        summed = frames[:, cols].astype(jnp.float32) + mixed
        out[:, cols] = jnp.where(pos < length, summed, 0.0).astype(jnp.bfloat16)
        stores.append(pltpu.make_async_copy(out.at[:, cols], out_hbm.at[:, cols], out_sem.at[n]))
        stores[-1].start()

    for copy in copies.values():
        copy.wait_send()
    for store in stores:
        store.wait()


def per_device(frames, lengths, ln_gain, w_query, w_key, w_value, w_out):
    vmem = pl.BlockSpec(memory_space=pltpu.VMEM)
    anywhere = pl.BlockSpec(memory_space=pl.ANY)
    bf16 = jnp.bfloat16
    result = pl.pallas_call(
        body,
        out_shape=jax.ShapeDtypeStruct((ROWS, D), bf16),
        in_specs=[pl.BlockSpec(memory_space=pltpu.SMEM), anywhere, vmem, vmem, vmem, vmem, vmem],
        out_specs=anywhere,
        scratch_shapes=[
            pltpu.VMEM((ROWS, D), bf16),
            pltpu.VMEM((ROWS, D), bf16),
            pltpu.VMEM((32, D), jnp.float32),
            pltpu.VMEM((2, 32, HALF), bf16),
            pltpu.VMEM((W, D), bf16),
            pltpu.VMEM((W, D), bf16),
            pltpu.VMEM((32, HALF), bf16),
            pltpu.VMEM((8, 16, HALF), bf16),
            pltpu.VMEM((8, 32, HALF), bf16),
            pltpu.VMEM((H, 2, HD, HALF), bf16),
            pltpu.VMEM((H, 2, 2 * HD, HALF), bf16),
            pltpu.VMEM((4, 16, HALF), bf16),
            pltpu.VMEM((2, 8, 4, 48, HALF), bf16),
            pltpu.VMEM((H, HD, D), bf16),
            pltpu.VMEM((D, EXT), bf16),
            pltpu.VMEM((H, HD, EXT), bf16),
            pltpu.VMEM((ROWS // W, 3 * W, W), jnp.float32),
            pltpu.VMEM((H, HD, ROWS), bf16),
            pltpu.SemaphoreType.DMA,
            pltpu.SemaphoreType.DMA((4,)),
            pltpu.SemaphoreType.DMA((N_COPIES,)),
            pltpu.SemaphoreType.DMA((N_COPIES,)),
        ],
        compiler_params=pltpu.CompilerParams(
            collective_id=0, has_side_effects=True, vmem_limit_bytes=60 * 2**20
        ),
    )(lengths, frames[0], ln_gain, w_key.T, w_value.T, w_query.T, w_out.T)
    return result[None]


def solution(mesh):
    in_specs = (
        P("dp", "tm", None),
        P("dp"),
        P(),
        P(None, ("dp", "tm")),
        P(None, ("dp", "tm")),
        P(None, ("dp", "tm")),
        P(None, ("dp", "tm")),
    )
    return jax.shard_map(
        per_device,
        mesh=mesh,
        in_specs=in_specs,
        out_specs=P("dp", "tm", None),
        check_vma=False,
    )
```

time: 105 us -> 90.7 us (0.86)
  Pallas kernels: 98.5 us -> 87.2 us
  local copies, waits for them, and re-layouts: 4.63 us -> 2.65 us
    pallas_call x1, Pallas kernels: 98.5 us -> 87.2 us  [per_device(): pl.pallas_call(body, out_shape=jax.ShapeDtypeStruct((ROWS, D), bf16), in_...]
    broadcast_in_dim x1 -> x0, local copies, waits for them, and re-layouts: 1.29 us -> none  [per_device(): ln_gain[None]]
where the time goes in v2:
time: 90.7 us; the launch traced here: 90.5 us
  Pallas kernels  87.2 us (96%)
  local copies, waits for them, and re-layouts  2.65 us (3%)
    pallas_call x1, Pallas kernels, per_device(): pl.pallas_call(body, out_shape=jax.ShapeDtypeStruct((ROWS, D), bf16), in_...  87.2 us
    unnamed x1, local copies, waits for them, and re-layouts  2.65 us

profile of v2, /device:TPU:1, one launch (start us, length us, event | category | flops | bytes accessed | tf_op | source)
XLA Modules:
  0.0 90.5 jit_solution(10503676703725933181)
XLA Ops:
  0.7 87.2 %shard_map.73 = bf16[512,1536]{1,0:T(8,128)(2,1)} custom-call(s32[1]{0:T(128)S(6)} %copy.9.len_ref, bf16[512,1536]{1,0:T(8,128)(2,1)} %bitcast.7, f32[1536]{0:T(1024)} %gain_ref.1, bf16[6,1536]{1,0:T(8,128)(2,1)} %bitcast.8, bf16[6,1536]{1,0:T(8,128)(2,1)} %bitcast.9, bf16[6,1536]{1,0:T(8,128)(2,1)} %bitcast.10, bf16[6,1536]{1,0:T(8,128)(2,1)} %bitcast.11), custom_call_target="tpu_custom_call" | custom-call | tf_op jit(solution)/shard_map/pallas_call | solution.py:407
  87.9 2.7 %copy.10 = bf16[1,512,1536]{2,1,0:T(8,128)(2,1)} copy(bf16[1,512,1536]{2,1,0:T(8,128)(2,1)} %bitcast.6) | data formatting | bytes 3145728

commit v3 on v2

--- a/solution.py
+++ b/solution.py
@@ -152,22 +152,44 @@
     oline[along] = jnp.concatenate([one[24:], two[24:]], axis=0)
     for k in LINE:
         send(f"of{k}", oline.at[along], oline.at[along], first_line[k])
-    zr[z] = jnp.concatenate([one[8:24], two[8:24]], axis=0)
+    row = lax.broadcasted_iota(jnp.int32, (24, 32), 0)
+    col = lax.broadcasted_iota(jnp.int32, (24, 32), 1)
+    order = jnp.where(col == (row // 6) * 8 + row % 6, 1.0, 0.0).astype(jnp.bfloat16)
+    packed = jnp.dot(
+        order,
+        jnp.concatenate([one[8:24], two[8:24]], axis=0),
+        preferred_element_type=jnp.float32,
+    )
+    zr[z, :, :HALF] = packed[:16].astype(jnp.bfloat16)
+    zr[z, :, HALF:] = jnp.concatenate(
+        [packed[16:, : HALF // 2], packed[16:, HALF // 2 :]], axis=0
+    ).astype(jnp.bfloat16)
     fetch.wait()
 
     norm_block(frames, 0, W)
     norm_block(frames, W, 2 * W)
 
-    def ordered(buf, kinds):
-        rows, cols = kinds * HD, 8 * kinds * 16
-        row = lax.broadcasted_iota(jnp.int32, (rows, cols), 0)
-        col = lax.broadcasted_iota(jnp.int32, (rows, cols), 1)
-        kind, unit, part = row // HD, (row % HD) // 6, row % 6
-        source = (unit // 2) * (kinds * 16) + (unit % 2) * (kinds * 8) + kind * 8 + part
+    def chosen(rows, source, buf):
+        col = lax.broadcasted_iota(jnp.int32, (rows, buf.shape[0]), 1)
         order = jnp.where(col == source, 1.0, 0.0).astype(jnp.bfloat16)
-        return jnp.dot(order, buf.reshape(cols, HALF), preferred_element_type=jnp.float32).astype(
-            jnp.bfloat16
-        )
+        return jnp.dot(order, buf, preferred_element_type=jnp.float32)
+
+    def ordered_keys():
+        row = lax.broadcasted_iota(jnp.int32, (HD, 8 * 16), 0)
+        source = (row // 12) * 16 + (row % 12 // 6) * 8 + row % 6
+        return chosen(HD, source, zk[...].reshape(8 * 16, HALF)).astype(jnp.bfloat16)
+
+    def ordered_rest():
+        row = lax.broadcasted_iota(jnp.int32, (2 * HD, 8 * 16), 0)
+        kind, chip, part = row // HD, (row % HD) // 12, row % 12
+        local = (part // 6) * 12 + kind * 6 + part % 6
+        base = chip * 16
+        wide = zr[:, :, :HALF].reshape(8 * 16, HALF)
+        tail = zr[:, :, HALF:].reshape(8 * 16, HALF // 2)
+        first = chosen(2 * HD, jnp.where(local < 16, base + local, -1), wide)
+        left = chosen(2 * HD, jnp.where(local < 16, -1, base + local - 16), tail)
+        right = chosen(2 * HD, jnp.where(local < 16, -1, base + local - 8), tail)
+        return (first + jnp.concatenate([left, right], axis=1)).astype(jnp.bfloat16)
 
     parts = (wk, wr)
 
@@ -286,7 +308,7 @@
     arrived(*(f"zk{k}" for k in z_line))
     for k, peer in z_line.items():
         send(f"zr{k}", zr.at[z], zr.at[z], peer)
-    wk[own, core] = ordered(zk[...], 1)
+    wk[own, core] = ordered_keys()
     begin(KEYS)
     arrived(*(f"of{k}" for k in LINE))
     row = lax.broadcasted_iota(jnp.int32, (48, 64), 0)
@@ -303,8 +325,16 @@
     second_begin(KEYS, -1)
     second_begin(KEYS, 1)
     norm_block(frames, 3 * W, 4 * W)
+    for t in range(ROWS // W):
+        key = lax.broadcasted_iota(jnp.int32, (3 * W, W), 0)
+        query = lax.broadcasted_iota(jnp.int32, (3 * W, W), 1)
+        key_pos = key + (first_pos + (t - 1) * W)
+        allowed = (
+            (key - query >= 0) & (key - query <= 2 * W) & (key_pos >= 0) & (key_pos < length)
+        )
+        bias[t] = jnp.where(allowed, 0.0, -1e9).astype(jnp.float32)
     arrived(*(f"zr{k}" for k in z_line))
-    wr[own, core] = ordered(zr[...], 2)
+    wr[own, core] = ordered_rest()
     begin(REST)
     send("low", frames_hbm.at[pl.ds(ROWS - W, W)], low, after)
     send("high", frames_hbm.at[pl.ds(0, W)], high, before)
@@ -312,50 +342,42 @@
     first_end(KEYS)
     second_begin(KEYS, 2)
     second_end(KEYS, 0)
-    for t in range(ROWS // W):
-        key = lax.broadcasted_iota(jnp.int32, (3 * W, W), 0)
-        query = lax.broadcasted_iota(jnp.int32, (3 * W, W), 1)
-        key_pos = key + (first_pos + (t - 1) * W)
-        allowed = (
-            (key - query >= 0) & (key - query <= 2 * W) & (key_pos >= 0) & (key_pos < length)
-        )
-        bias[t] = jnp.where(allowed, 0.0, -1e9).astype(jnp.float32)
+    second_step(KEYS, -1)
+    second_step(KEYS, 1)
     arrived("low", "high")
     norm_block(low, 0, 0)
     norm_block(high, 0, W + ROWS)
-    second_step(KEYS, -1)
-    second_step(KEYS, 1)
-    o_ring(1, 0)
+    second_step(KEYS, 2)
+    second_end(KEYS, -1)
+    second_end(KEYS, 1)
     keys((0, 0), (-1, 0), (1, 0), (0, -1), (0, 1), (2, 0))
-    o_ring(1, 1)
     first_step(REST)
     second_step(REST, 0)
     second_begin(REST, -1)
     second_begin(REST, 1)
-    second_step(KEYS, 2)
-    second_end(KEYS, -1)
-    second_end(KEYS, 1)
+    o_ring(1, 0)
     heads((0, 0))
-    o_ring(2, 0)
+    second_end(KEYS, 2)
+    o_ring(1, 1)
     keys((0, 2), (-1, -1), (1, 1), (-1, 1))
-    second_end(KEYS, 2)
-    o_ring(2, 1)
     first_end(REST)
     second_begin(REST, 2)
     second_end(REST, 0)
+    o_ring(2, 0)
     heads((-1, 0), (1, 0))
+    o_ring(2, 1)
+    second_step(REST, -1)
+    heads((0, -1), (0, 1))
+    second_step(REST, 1)
     o_ring(3, 0)
-    heads((0, -1), (0, 1))
-    second_step(REST, -1)
+    heads((2, 0), (0, 2))
     o_ring(3, 1)
+    second_end(REST, -1)
     keys((1, -1), (2, -1), (2, 1), (-1, 2), (1, 2), (2, 2))
-    second_step(REST, 1)
-    heads((2, 0), (0, 2))
+    second_step(REST, 2)
+    heads((-1, -1), (1, 1))
+    second_end(REST, 1)
     o_end()
-    second_end(REST, -1)
-    heads((-1, -1), (1, 1))
-    second_step(REST, 2)
-    second_end(REST, 1)
     heads((-1, 1), (1, -1))
     arrived(*(f"oc{k}" for k in range(-3, 5)))
     row = lax.broadcasted_iota(jnp.int32, (4 * HD, 8 * 48), 0)
@@ -418,7 +440,7 @@
             pltpu.VMEM((W, D), bf16),
             pltpu.VMEM((32, HALF), bf16),
             pltpu.VMEM((8, 16, HALF), bf16),
-            pltpu.VMEM((8, 32, HALF), bf16),
+            pltpu.VMEM((8, 16, 3 * HALF // 2), bf16),
             pltpu.VMEM((H, 2, HD, HALF), bf16),
             pltpu.VMEM((H, 2, 2 * HD, HALF), bf16),
             pltpu.VMEM((4, 16, HALF), bf16),

time: 90.7 us -> 89.3 us (0.985)
  Pallas kernels: 87.2 us -> 85.8 us
    pallas_call x1, Pallas kernels: 87.2 us -> 85.8 us  [per_device(): pl.pallas_call(body, out_shape=jax.ShapeDtypeStruct((ROWS, D), bf16), in_...]
where the time goes in v3:
time: 89.3 us; the launch traced here: 89.1 us
  Pallas kernels  85.8 us (96%)
  local copies, waits for them, and re-layouts  2.65 us (3%)
    pallas_call x1, Pallas kernels, per_device(): pl.pallas_call(body, out_shape=jax.ShapeDtypeStruct((ROWS, D), bf16), in_...  85.8 us
    unnamed x1, local copies, waits for them, and re-layouts  2.65 us

profile of v3, /device:TPU:1, one launch (start us, length us, event | category | flops | bytes accessed | tf_op | source)
XLA Modules:
  0.0 89.1 jit_solution(7353255629014750739)
XLA Ops:
  0.7 85.8 %shard_map.73 = bf16[512,1536]{1,0:T(8,128)(2,1)} custom-call(s32[1]{0:T(128)S(6)} %copy.9.len_ref, bf16[512,1536]{1,0:T(8,128)(2,1)} %bitcast.7, f32[1536]{0:T(1024)} %gain_ref.1, bf16[6,1536]{1,0:T(8,128)(2,1)} %bitcast.8, bf16[6,1536]{1,0:T(8,128)(2,1)} %bitcast.9, bf16[6,1536]{1,0:T(8,128)(2,1)} %bitcast.10, bf16[6,1536]{1,0:T(8,128)(2,1)} %bitcast.11), custom_call_target="tpu_custom_call" | custom-call | tf_op jit(solution)/shard_map/pallas_call | solution.py:429
  86.5 2.7 %copy.10 = bf16[1,512,1536]{2,1,0:T(8,128)(2,1)} copy(bf16[1,512,1536]{2,1,0:T(8,128)(2,1)} %bitcast.6) | data formatting | bytes 3145728

commit v4 on v3

--- a/solution.py
+++ b/solution.py
@@ -379,6 +379,9 @@
     second_end(REST, 1)
     o_end()
     heads((-1, 1), (1, -1))
+    heads((2, -1), (-1, 2))
+    second_end(REST, 2)
+    heads((2, 1), (1, 2))
     arrived(*(f"oc{k}" for k in range(-3, 5)))
     row = lax.broadcasted_iota(jnp.int32, (4 * HD, 8 * 48), 0)
     col = lax.broadcasted_iota(jnp.int32, (4 * HD, 8 * 48), 1)
@@ -395,9 +398,6 @@
                 px, py = (fixed, k) if half else (k, fixed)
                 head = px * 4 + (py % 2) * 2 + py // 2
                 wo[head, :, half * HALF : (half + 1) * HALF] = four[k * HD : (k + 1) * HD]
-    heads((2, -1), (-1, 2))
-    second_end(REST, 2)
-    heads((2, 1), (1, 2))
     heads((2, 2))
 
     att_rows = att[...].reshape(D, ROWS).T

time: 89.3 us -> 88.1 us (0.987); the launches traced: 89.1 us -> 86.3 us
  Pallas kernels: 85.8 us -> 83 us
    pallas_call x1, Pallas kernels: 85.8 us -> 83 us  [per_device(): pl.pallas_call(body, out_shape=jax.ShapeDtypeStruct((ROWS, D), bf16), in_...]
where the time goes in v4:
time: 88.1 us; the launch traced here: 86.3 us
  Pallas kernels  83 us (94%)
  local copies, waits for them, and re-layouts  2.65 us (3%)
    pallas_call x1, Pallas kernels, per_device(): pl.pallas_call(body, out_shape=jax.ShapeDtypeStruct((ROWS, D), bf16), in_...  83 us
    unnamed x1, local copies, waits for them, and re-layouts  2.65 us

profile of v4, /device:TPU:1, one launch (start us, length us, event | category | flops | bytes accessed | tf_op | source)
XLA Modules:
  0.0 86.3 jit_solution(10686151892333693421)
XLA Ops:
  0.7 83.0 %shard_map.73 = bf16[512,1536]{1,0:T(8,128)(2,1)} custom-call(s32[1]{0:T(128)S(6)} %copy.9.len_ref, bf16[512,1536]{1,0:T(8,128)(2,1)} %bitcast.7, f32[1536]{0:T(1024)} %gain_ref.1, bf16[6,1536]{1,0:T(8,128)(2,1)} %bitcast.8, bf16[6,1536]{1,0:T(8,128)(2,1)} %bitcast.9, bf16[6,1536]{1,0:T(8,128)(2,1)} %bitcast.10, bf16[6,1536]{1,0:T(8,128)(2,1)} %bitcast.11), custom_call_target="tpu_custom_call" | custom-call | tf_op jit(solution)/shard_map/pallas_call | solution.py:429
  83.7 2.7 %copy.10 = bf16[1,512,1536]{2,1,0:T(8,128)(2,1)} copy(bf16[1,512,1536]{2,1,0:T(8,128)(2,1)} %bitcast.6) | data formatting | bytes 3145728
